TPU v7x, 32 devices: a whole 2x2x4 slice. The times are simulated.
32 devices in a mesh: blk: 8 (over z, x), frq: 4 (over y, core).
Axes of the slice: x: 2, y: 2, z: 4, core: 2. Of those that a mesh axis runs over, the one named last changes fastest.
Arguments:
- spectra: bfloat16 [2, 3, 128, 512], P(None, None, 'blk', 'frq'), may hold values from -6 to 6
- observed: bfloat16 [128, 3, 3, 1024], P(('blk', 'frq')), may hold values from -6 to 6
- own_station: int32 [8, 8, 2], P('blk'), may hold values from 0 to 15
- partner_station: int32 [8, 8, 2], P('blk'), may hold values from 0 to 15, as said below
- pair_count: int32 [8, 8], P('blk'), may hold values from 1 to 2, as said below
Outputs:
- adjoint: float32 [1024, 3, 128], P('frq', None, 'blk')
Inputs may be any that keep to these rules, and one draw needn't show every extreme that they name: `partner_station`: within the reading block's own block pair, a slot's two stations differ. `pair_count`: the live slots of a block pair are its first ones; every reading block has a block pair with all 2 slots live.
All inputs are finite; a program needn't handle non-finite values.
Results may differ from a plain program's by a relative error of at most 0.003.
Values may be sent and summed in bfloat16 or wider, within the bound.
A program may use at most 64 MiB of HBM per device.

v0:
```python
import functools
import math

import jax
import jax.numpy as jnp
import ml_dtypes
import numpy as np
from jax import lax
from jax.experimental import pallas as pl
from jax.experimental.pallas import tpu as pltpu
from jax.sharding import PartitionSpec as P

NF = 512
NT = 1024
LAG = NT // 4
MESH = pl.DeviceIdType.MESH
BF = jnp.bfloat16
F32 = jnp.float32


def tables():
    freq = np.arange(NF, dtype=np.int64)
    time = np.arange(NT, dtype=np.int64)
    num = (2 * freq + 1)[:, None] * time[None, :] % (2 * NT)
    phase = num.astype(np.float32) * np.float32(math.pi / NT)
    scale = np.float32(math.sqrt(NF))
    full = np.concatenate([np.cos(phase) / scale, -(np.sin(phase) / scale)], axis=0)
    high = full.astype(ml_dtypes.bfloat16)
    kept = np.concatenate([high[:, :LAG], high[:, NT - LAG :]], axis=1)
    return high, np.ascontiguousarray(kept.T)


def loop(count, body):
    if count <= 8:
        for step in range(count):
            body(step)
    else:

        def wrapped(step, carry):
            body(step)
            return carry

        lax.fori_loop(0, count, wrapped, 0)


def kernel(
    n_b, n_q, cap, sta, item, scale,
    spec_ref, obs_ref, own_in, part_in, cnt_in, high_ref, kept_ref,
    out_ref,
    own_ref, part_ref, cnt_ref, spec, obs, high, kept, obsf,
    g_send, g_recv, g_own, own_send, own_recv, row_send, row_recv,
    far_send, far_recv, ownt_send, ownt_recv,
    local_sem, g_ss, g_rs, own_ss, own_rs, row_ss, row_rs, far_ss, far_rs, ownt_ss, ownt_rs,
):
    per = n_b // n_q
    rows = cap * 8
    cols = 8 * sta
    band = NF // n_q
    half = NT // n_q // 2
    chunk = min(item, 16)
    chunks = item // chunk
    prow = -(-9 * chunk // 16) * 16
    blocks = chunk // cap
    bits = chunk.bit_length() - 1
    b = lax.axis_index("blk")
    q = lax.axis_index("frq")
    home = lax.div(b, per)
    slot_in = lax.rem(b, per)

    def wrap(value, size):
        return jnp.where(value >= size, value - size, value)

    id_loads = [
        pltpu.make_async_copy(part_in, part_ref, local_sem.at[5]),
        pltpu.make_async_copy(own_in, own_ref, local_sem.at[6]),
        pltpu.make_async_copy(cnt_in, cnt_ref, local_sem.at[7]),
    ]
    for load in id_loads:
        load.start()
    loads = [
        pltpu.make_async_copy(spec_ref.at[0], spec.at[0, pl.ds(0, 3)], local_sem.at[0]),
        pltpu.make_async_copy(spec_ref.at[1], spec.at[1, pl.ds(0, 3)], local_sem.at[1]),
        pltpu.make_async_copy(obs_ref, obs, local_sem.at[2]),
        pltpu.make_async_copy(
            high_ref.at[pl.ds(0, NF)], high.at[pl.ds(0, NF)], local_sem.at[3]
        ),
        pltpu.make_async_copy(
            high_ref.at[pl.ds(NF, NF)], high.at[pl.ds(NF, NF)], local_sem.at[4]
        ),
        pltpu.make_async_copy(kept_ref, kept, local_sem.at[8]),
    ]
    for load in loads[:3]:
        load.start()

    barrier = pltpu.get_barrier_semaphore()

    def greet(step):
        pl.semaphore_signal(
            barrier, inc=1, device_id=(wrap(b + 1 + step, n_b), q), device_id_type=MESH
        )

    for step in range(n_q - 1):
        pl.semaphore_signal(
            barrier, inc=1, device_id=(b, wrap(q + 1 + step, n_q)), device_id_type=MESH
        )
    loop(n_b - 1, greet)

    row_i = lax.broadcasted_iota(jnp.int32, (rows, cols), 0)
    col_i = lax.broadcasted_iota(jnp.int32, (rows, cols), 1)
    row_s = row_i >> 3
    base = col_i - (row_i & 7) * sta

    def pick(ids, block):
        chosen = jnp.full((rows, cols), ids[0, block], jnp.int32)
        for s in range(1, cap):
            chosen = jnp.where(row_s == s, ids[s, block], chosen)
        return jnp.where(base == chosen, 1.0, 0.0).astype(BF)

    def build(block):
        g_send[block] = pick(part_ref, block)
        g_own[block] = pick(own_ref, block)

    for load in id_loads:
        load.wait()
    loop(n_b, build)
    spec[0, 3] = jnp.zeros((sta, band), BF)
    spec[1, 3] = jnp.zeros((sta, band), BF)
    pl.semaphore_wait(barrier, n_b + n_q - 2)

    def many(src, dst, count, send_sem, recv_sem):
        return pltpu.make_async_remote_copy(
            src_ref=src.at[pl.ds(0, count)], dst_ref=dst.at[pl.ds(0, count)], send_sem=send_sem,
            recv_sem=recv_sem, device_id=(wrap(b + 1, n_b), q), device_id_type=MESH,
        )

    def wait_block(copy_of, wait):
        @pl.when(q == home)
        def _():
            wait(copy_of(n_b - 1))

        @pl.when(q != home)
        def _():
            wait(copy_of(n_b))

    def g_copy(block, slot):
        return pltpu.make_async_remote_copy(
            src_ref=g_send.at[block], dst_ref=g_recv.at[slot], send_sem=g_ss,
            recv_sem=g_rs, device_id=(block, q), device_id_type=MESH,
        )

    def g_start(step):
        block = wrap(b + 1 + step, n_b)
        g_copy(block, b).start()

    loop(n_b - 1, g_start)
    g_recv[b] = g_send[b]

    loads[0].wait()
    loads[1].wait()
    station_rows = spec[...].reshape(cols, band)

    def own_copy(peer, slot):
        return pltpu.make_async_remote_copy(
            src_ref=own_send.at[peer], dst_ref=own_recv.at[slot], send_sem=own_ss,
            recv_sem=own_rs, device_id=(b, peer), device_id_type=MESH,
        )

    picked = jnp.dot(
        g_own[...].reshape(n_b * rows, cols), station_rows, preferred_element_type=F32
    ).astype(BF)
    own_send[...] = picked.reshape(n_q, item * 8, band)
    for step in range(n_q - 1):
        own_copy(wrap(q + 1 + step, n_q), q).start()
    own_recv[q] = own_send[q]
    for load in loads[3:]:
        load.start()

    p_i = lax.broadcasted_iota(jnp.int32, (prow, 1), 0)
    p_ae = p_i >> bits
    p_slot = p_i & (chunk - 1)
    p_a = sum((p_ae >= 3 * m).astype(jnp.int32) for m in (1, 2, 3))
    p_e = jnp.where(p_ae >= 9, 3, p_ae - 3 * p_a)
    e_col = lax.broadcasted_iota(jnp.int32, (prow, chunk * 8), 1)

    def expand(component):
        want = p_slot * 8 + component
        return jnp.concatenate(
            [jnp.where(e_col == want + 4 * ri, 1.0, 0.0) for ri in range(2)], axis=0
        ).astype(BF)

    expand_u = expand(p_a)
    expand_v = expand(p_e)
    s_row = lax.broadcasted_iota(jnp.int32, (chunk * 8, prow), 0)
    s_col = lax.broadcasted_iota(jnp.int32, (chunk * 8, prow), 1)
    s_ae = s_col >> bits
    s_a = sum((s_ae >= 3 * m).astype(jnp.int32) for m in (1, 2, 3))
    s_e = jnp.where(s_ae >= 9, 3, s_ae - 3 * s_a)
    s_same = (s_row >> 3) == (s_col & (chunk - 1))
    s_comp = s_row & 3
    sum_e = jnp.where(s_same & (s_a == s_comp), 1.0, 0.0).astype(BF)
    sum_a = jnp.where(s_same & (s_e == s_comp), 1.0, 0.0).astype(BF)
    lane = lax.broadcasted_iota(jnp.int32, (prow, 2 * LAG), 1)
    lag = jnp.where(lane < LAG, lane, 2 * LAG - lane)
    in_window = (lag >= NT // 32) & (lag < NT // 4)

    def prepare(at):
        if prow > 9 * chunk:
            obsf[9 * chunk :, :] = jnp.zeros((prow - 9 * chunk, 2 * LAG), F32)
        for a in range(3):
            for e in range(3):
                slab = obs[a, e, pl.ds(at * chunk, chunk), :] if chunks > 1 else obs[a, e]
                at_row = (3 * a + e) * chunk
                obsf[at_row : at_row + chunk, :LAG] = slab[:, :LAG].astype(F32)
                obsf[at_row : at_row + chunk, LAG:] = slab[:, NT - LAG :].astype(F32)

    loads[2].wait()
    if chunks == 1:
        prepare(0)

    many(g_send, g_recv, n_b - 1, g_ss, g_rs).wait_recv()
    row_send[...] = jnp.dot(
        g_recv[...].reshape(n_b * rows, cols), station_rows, preferred_element_type=F32
    ).astype(BF).reshape(n_b, rows, band)

    def row_copy(block, slot):
        return pltpu.make_async_remote_copy(
            src_ref=row_send.at[block], dst_ref=row_recv.at[slot], send_sem=row_ss,
            recv_sem=row_rs, device_id=(block, home), device_id_type=MESH,
        )

    mine = q * per + slot_in

    def row_start(step):
        row_copy(wrap(b + 1 + step, n_b), mine).start()

    loop(n_b - 1, row_start)

    @pl.when(q != home)
    def _():
        row_copy(b, mine).start()

    @pl.when(q == home)
    def _():
        row_recv[mine] = row_send[b]

    many(own_send, own_recv, n_q - 1, own_ss, own_rs).wait_recv()

    def spread(matrix, parts):
        outs = [jnp.dot(matrix, part, preferred_element_type=F32) for part in parts]
        both = jnp.concatenate(outs, axis=1)
        return both[:prow], both[prow:]

    def spread_own(at):
        return spread(
            expand_u,
            [own_recv[p, pl.ds(at * chunk * 8, chunk * 8), :] for p in range(n_q)],
        )

    early = spread_own(0) if chunks == 1 else None
    wait_block(
        lambda count: many(row_send, row_recv, count, row_ss, row_rs), lambda c: c.wait_recv()
    )
    for load in loads[3:]:
        load.wait()

    def far_copy(peer, inner, slot):
        return pltpu.make_async_remote_copy(
            src_ref=far_send.at[peer * per + inner], dst_ref=far_recv.at[slot],
            send_sem=far_ss, recv_sem=far_rs,
            device_id=(q * per + inner, peer), device_id_type=MESH,
        )

    def ownt_copy(peer, slot):
        return pltpu.make_async_remote_copy(
            src_ref=ownt_send.at[peer], dst_ref=ownt_recv.at[slot], send_sem=ownt_ss,
            recv_sem=ownt_rs, device_id=(b, peer), device_id_type=MESH,
        )

    def send_quarter(peer):
        def far_start(inner):
            other = jnp.logical_or(q * per + inner != b, q != peer)

            @pl.when(other)
            def _():
                far_copy(peer, inner, b).start()

            @pl.when(jnp.logical_not(other))
            def _():
                far_recv[b] = far_send[peer * per + inner]

        loop(per, far_start)

        @pl.when(q != peer)
        def _():
            ownt_copy(peer, q).start()

        @pl.when(q == peer)
        def _():
            ownt_recv[peer] = ownt_send[peer]

    def work(at):
        if chunks > 1:
            prepare(at)
        alive = jnp.zeros((prow, 1), jnp.int32)
        for i in range(chunk):
            count = cnt_ref[0, q * per + at * blocks + i // cap]
            live = jnp.clip(count - i % cap, 0, 1)
            alive = jnp.where(p_slot == i, live, alive)
        alive = jnp.where(p_ae < 9, alive, 0)
        alive_f = alive.astype(F32)

        ur, ui = early if chunks == 1 else spread_own(at)
        vr, vi = spread(
            expand_v,
            [
                row_recv[pl.ds(p * per + at * blocks, blocks)].reshape(chunk * 8, band)
                for p in range(n_q)
            ],
        )
        cross = jnp.concatenate(
            [(ur * vr + ui * vi) * alive_f, (ui * vr - ur * vi) * alive_f], axis=1
        ).astype(BF)
        correlation = jnp.concatenate(
            [
                jnp.dot(cross, high[:, :LAG], preferred_element_type=F32),
                jnp.dot(cross, high[:, NT - LAG :], preferred_element_type=F32),
            ],
            axis=1,
        )
        residual = jnp.where(
            in_window & (alive > 0), correlation - obsf[...], 0.0
        ).astype(BF)
        adj = jnp.dot(residual, kept[...], preferred_element_type=F32).astype(BF).astype(F32)
        ar, ai = adj[:, :NF], adj[:, NF:]

        def reduce(matrix, real, imag):
            terms = jnp.concatenate([real, imag], axis=1)
            top = terms.astype(BF)
            rest = (terms - top.astype(F32)).astype(BF)
            return jnp.dot(matrix, top, preferred_element_type=F32) + jnp.dot(
                matrix, rest, preferred_element_type=F32
            )

        grad = jnp.concatenate(
            [
                reduce(sum_e, ar * vr - ai * vi, ar * vi + ai * vr),
                reduce(sum_a, ar * ur + ai * ui, ar * ui - ai * ur),
            ],
            axis=0,
        )
        top = grad.astype(BF)
        rest = (grad - top.astype(F32)).astype(BF)
        stacked = jnp.concatenate([top, rest], axis=0)
        count = chunk * 16
        first_half = (lax.broadcasted_iota(jnp.int32, (count, half), 0) & 7) < 4
        for peer in range(n_q):
            at_col = peer * 2 * half
            product = jnp.dot(
                stacked, high[:, at_col : at_col + 2 * half], preferred_element_type=F32
            )
            product = (product[:count] + product[count:]) * scale
            message = jnp.where(first_half, product[:, :half], product[:, half:])
            ownt_send[peer, pl.ds(at * chunk * 8, chunk * 8), :] = message[: chunk * 8]
            far_send[pl.ds(peer * per + at * blocks, blocks)] = (
                message[chunk * 8 :].astype(BF).reshape(blocks, rows, half)
            )
            if chunks == 1:
                send_quarter(peer)

    if chunks == 1:
        work(0)
    else:

        def work_step(at, carry):
            work(at)
            return carry

        lax.fori_loop(0, chunks, work_step, 0)
        for peer in range(n_q):
            send_quarter(peer)

    def scatter(matrix, values):
        return lax.dot_general(
            matrix, values, (((0,), (0,)), ((), ())), preferred_element_type=F32
        )

    many(ownt_send, ownt_recv, n_q - 1, ownt_ss, ownt_rs).wait_recv()
    own_time = ownt_recv[...].reshape(n_q * item * 8, half)
    own_top = own_time.astype(BF)
    own_rest = (own_time - own_top.astype(F32)).astype(BF)
    g_mine = g_own[...].reshape(n_b * rows, cols)
    own_sum = scatter(g_mine, own_top) + scatter(g_mine, own_rest)
    wait_block(
        lambda count: many(far_send, far_recv, count, far_ss, far_rs), lambda c: c.wait_recv()
    )
    summed = own_sum + scatter(
        g_recv[...].reshape(n_b * rows, cols), far_recv[...].reshape(n_b * rows, half)
    )
    for h in range(2):
        at_row = h * 4 * sta
        out_ref[:, :, h * half : (h + 1) * half] = summed[at_row : at_row + 3 * sta].reshape(
            3, sta, half
        )

    many(g_send, g_recv, n_b - 1, g_ss, g_rs).wait_send()
    many(own_send, own_recv, n_q - 1, own_ss, own_rs).wait_send()
    many(ownt_send, ownt_recv, n_q - 1, ownt_ss, ownt_rs).wait_send()
    wait_block(
        lambda count: many(row_send, row_recv, count, row_ss, row_rs), lambda c: c.wait_send()
    )
    wait_block(
        lambda count: many(far_send, far_recv, count, far_ss, far_rs), lambda c: c.wait_send()
    )


def local(spectra, observed, own_station, partner_station, pair_count):
    n_b = lax.axis_size("blk")
    n_q = lax.axis_size("frq")
    sta = spectra.shape[2]
    band = spectra.shape[3]
    cap = own_station.shape[2]
    item = observed.shape[0]
    per = n_b // n_q
    rows = cap * 8
    cols = 8 * sta
    half = NT // n_q // 2
    chunk = min(item, 16)
    prow = -(-9 * chunk // 16) * 16
    scale = 1.0 / math.sqrt(2.0 * n_b * cap / sta)
    high, kept = tables()
    dma = pltpu.SemaphoreType.DMA
    held = pl.BlockSpec(memory_space=pltpu.HBM)
    out = pl.pallas_call(
        functools.partial(kernel, n_b, n_q, cap, sta, item, scale),
        out_shape=jax.ShapeDtypeStruct((3, sta, 2 * half), F32),
        in_specs=[held] * 7,
        out_specs=pl.BlockSpec(memory_space=pltpu.VMEM),
        scratch_shapes=[
            pltpu.SMEM((cap, n_b), jnp.int32),
            pltpu.SMEM((cap, n_b), jnp.int32),
            pltpu.SMEM((1, n_b), jnp.int32),
            pltpu.VMEM((2, 4, sta, band), BF),
            pltpu.VMEM((3, 3, item, NT), BF),
            pltpu.VMEM(high.shape, BF),
            pltpu.VMEM(kept.shape, BF),
            pltpu.VMEM((prow, 2 * LAG), F32),
            pltpu.VMEM((n_b, rows, cols), BF),
            pltpu.VMEM((n_b, rows, cols), BF),
            pltpu.VMEM((n_b, rows, cols), BF),
            pltpu.VMEM((n_q, item * 8, band), BF),
            pltpu.VMEM((n_q, item * 8, band), BF),
            pltpu.VMEM((n_b, rows, band), BF),
            pltpu.VMEM((n_q * per, rows, band), BF),
            pltpu.VMEM((n_q * per, rows, half), BF),
            pltpu.VMEM((n_b, rows, half), BF),
            pltpu.VMEM((n_q, item * 8, half), F32),
            pltpu.VMEM((n_q, item * 8, half), F32),
            dma((9,)),
            *[dma(())] * 10,
        ],
        compiler_params=pltpu.CompilerParams(
            collective_id=0, has_side_effects=True, vmem_limit_bytes=32 * 1024 * 1024
        ),
        cost_estimate=pl.CostEstimate(flops=400_000_000, bytes_accessed=6_000_000, transcendentals=0),
    )(
        *(
            pltpu.with_memory_space_constraint(operand, pltpu.HBM)
            for operand in (
                spectra,
                jnp.transpose(observed, (1, 2, 0, 3)),
                jnp.transpose(own_station[0], (1, 0)),
                jnp.transpose(partner_station[0], (1, 0)),
                pair_count,
                jnp.asarray(high),
                jnp.asarray(kept),
            )
        )
    )
    return jnp.transpose(out, (2, 0, 1))


def solution(mesh):
    return jax.shard_map(
        local,
        mesh=mesh,
        in_specs=(
            P(None, None, "blk", "frq"),
            P(("blk", "frq"), None, None, None),
            P("blk", None, None),
            P("blk", None, None),
            P("blk", None),
        ),
        out_specs=P("frq", None, "blk"),
        check_vma=False,
    )
```

profile of v0, /device:TPU:0, one launch (start us, length us, event | category | flops | bytes accessed | tf_op | source)
XLA Modules:
  0.0 19.7 jit_solution(7416713508349237381)
XLA Ops:
  0.0 19.1 %shard_map.73 = f32[3,16,256]{2,1,0:T(8,128)S(1)} custom-call(bf16[2,3,16,128]{3,2,1,0:T(8,128)(2,1)} %spec_ref.1, bf16[3,3,4,1024]{3,2,1,0:T(4,128)(2,1)} %bitcast.9, s32[2,8]{1,0:T(2,128)} %bitcast.10, s32[2,8]{1,0:T(2,128)} %bitcast.11, s32[1,8]{1,0:T(1,128)} %cnt_in.1, bf16[1024,1024]{1,0:T(8,128)(2,1)} %constant.4.clone.high_ref, ...), custom_call_target="tpu_custom_call" | custom-call | flops 400000000 | bytes 6000000 | tf_op jit(solution)/shard_map/pallas_call | solution.py:433
  19.1 0.6 %copy.9 = f32[256,3,16]{0,2,1:T(8,128)} copy(f32[256,3,16]{0,2,1:T(8,128)S(1)} %bitcast.8) | data formatting | bytes 98304
where the time goes:
time: 19.9 us; the launch traced here: 19.7 us
  Pallas kernels  19.1 us (96%)
  local copies, waits for them, and re-layouts  0.62 us (3%)
    pallas_call x1, Pallas kernels, local(): pl.pallas_call(functools.partial(kernel, n_b, n_q, cap, sta, item, scale)...  19.1 us
    unnamed x1, local copies, waits for them, and re-layouts  0.62 us

commit v1 on v0

--- a/solution.py
+++ b/solution.py
@@ -48,7 +48,7 @@
     spec_ref, obs_ref, own_in, part_in, cnt_in, high_ref, kept_ref,
     out_ref,
     own_ref, part_ref, cnt_ref, spec, obs, high, kept, obsf,
-    g_send, g_recv, g_own, own_send, own_recv, row_send, row_recv,
+    g_send, g_recv, g_own, g_turn, own_send, own_recv, row_send, row_recv,
     far_send, far_recv, ownt_send, ownt_recv,
     local_sem, g_ss, g_rs, own_ss, own_rs, row_ss, row_rs, far_ss, far_rs, ownt_ss, ownt_rs,
 ):
@@ -89,9 +89,6 @@
         ),
         pltpu.make_async_copy(kept_ref, kept, local_sem.at[8]),
     ]
-    for load in loads[:3]:
-        load.start()
-
     barrier = pltpu.get_barrier_semaphore()
 
     def greet(step):
@@ -104,6 +101,8 @@
             barrier, inc=1, device_id=(b, wrap(q + 1 + step, n_q)), device_id_type=MESH
         )
     loop(n_b - 1, greet)
+    for load in loads:
+        load.start()
 
     row_i = lax.broadcasted_iota(jnp.int32, (rows, cols), 0)
     col_i = lax.broadcasted_iota(jnp.int32, (rows, cols), 1)
@@ -118,13 +117,13 @@
 
     def build(block):
         g_send[block] = pick(part_ref, block)
+
+    def build_own(block):
         g_own[block] = pick(own_ref, block)
 
     for load in id_loads:
         load.wait()
     loop(n_b, build)
-    spec[0, 3] = jnp.zeros((sta, band), BF)
-    spec[1, 3] = jnp.zeros((sta, band), BF)
     pl.semaphore_wait(barrier, n_b + n_q - 2)
 
     def many(src, dst, count, send_sem, recv_sem):
@@ -155,6 +154,9 @@
     loop(n_b - 1, g_start)
     g_recv[b] = g_send[b]
 
+    loop(n_b, build_own)
+    spec[0, 3] = jnp.zeros((sta, band), BF)
+    spec[1, 3] = jnp.zeros((sta, band), BF)
     loads[0].wait()
     loads[1].wait()
     station_rows = spec[...].reshape(cols, band)
@@ -172,8 +174,6 @@
     for step in range(n_q - 1):
         own_copy(wrap(q + 1 + step, n_q), q).start()
     own_recv[q] = own_send[q]
-    for load in loads[3:]:
-        load.start()
 
     p_i = lax.broadcasted_iota(jnp.int32, (prow, 1), 0)
     p_ae = p_i >> bits
@@ -197,8 +197,16 @@
     s_e = jnp.where(s_ae >= 9, 3, s_ae - 3 * s_a)
     s_same = (s_row >> 3) == (s_col & (chunk - 1))
     s_comp = s_row & 3
-    sum_e = jnp.where(s_same & (s_a == s_comp), 1.0, 0.0).astype(BF)
-    sum_a = jnp.where(s_same & (s_e == s_comp), 1.0, 0.0).astype(BF)
+    sum_e = jnp.where(s_same & (s_a == s_comp), 1.0, 0.0)
+    sum_a = jnp.where(s_same & (s_e == s_comp), 1.0, 0.0)
+    none = jnp.zeros((chunk * 8, prow), F32)
+    sums = jnp.concatenate(
+        [
+            jnp.concatenate([sum_e, sum_e, none, none], axis=1),
+            jnp.concatenate([none, none, sum_a, sum_a], axis=1),
+        ],
+        axis=0,
+    ).astype(BF)
     lane = lax.broadcasted_iota(jnp.int32, (prow, 2 * LAG), 1)
     lag = jnp.where(lane < LAG, lane, 2 * LAG - lane)
     in_window = (lag >= NT // 32) & (lag < NT // 4)
@@ -243,11 +251,22 @@
     def _():
         row_recv[mine] = row_send[b]
 
+    turn_i = lax.broadcasted_iota(jnp.int32, (cols, cols), 0)
+    turn_j = lax.broadcasted_iota(jnp.int32, (cols, cols), 1)
+    eye = jnp.where(turn_i == turn_j, 1.0, 0.0).astype(BF)
+
+    def turned(matrix):
+        return lax.dot_general(
+            eye, matrix[...].reshape(n_b * rows, cols), (((1,), (1,)), ((), ())),
+            preferred_element_type=F32,
+        ).astype(BF)
+
+    g_turn[0] = turned(g_recv)
+    g_turn[1] = turned(g_own)
     many(own_send, own_recv, n_q - 1, own_ss, own_rs).wait_recv()
 
     def spread(matrix, parts):
-        outs = [jnp.dot(matrix, part, preferred_element_type=F32) for part in parts]
-        both = jnp.concatenate(outs, axis=1)
+        both = jnp.dot(matrix, jnp.concatenate(parts, axis=1), preferred_element_type=F32)
         return both[:prow], both[prow:]
 
     def spread_own(at):
@@ -256,51 +275,7 @@
             [own_recv[p, pl.ds(at * chunk * 8, chunk * 8), :] for p in range(n_q)],
         )
 
-    early = spread_own(0) if chunks == 1 else None
-    wait_block(
-        lambda count: many(row_send, row_recv, count, row_ss, row_rs), lambda c: c.wait_recv()
-    )
-    for load in loads[3:]:
-        load.wait()
-
-    def far_copy(peer, inner, slot):
-        return pltpu.make_async_remote_copy(
-            src_ref=far_send.at[peer * per + inner], dst_ref=far_recv.at[slot],
-            send_sem=far_ss, recv_sem=far_rs,
-            device_id=(q * per + inner, peer), device_id_type=MESH,
-        )
-
-    def ownt_copy(peer, slot):
-        return pltpu.make_async_remote_copy(
-            src_ref=ownt_send.at[peer], dst_ref=ownt_recv.at[slot], send_sem=ownt_ss,
-            recv_sem=ownt_rs, device_id=(b, peer), device_id_type=MESH,
-        )
-
-    def send_quarter(peer):
-        def far_start(inner):
-            other = jnp.logical_or(q * per + inner != b, q != peer)
-
-            @pl.when(other)
-            def _():
-                far_copy(peer, inner, b).start()
-
-            @pl.when(jnp.logical_not(other))
-            def _():
-                far_recv[b] = far_send[peer * per + inner]
-
-        loop(per, far_start)
-
-        @pl.when(q != peer)
-        def _():
-            ownt_copy(peer, q).start()
-
-        @pl.when(q == peer)
-        def _():
-            ownt_recv[peer] = ownt_send[peer]
-
-    def work(at):
-        if chunks > 1:
-            prepare(at)
+    def first_part(at):
         alive = jnp.zeros((prow, 1), jnp.int32)
         for i in range(chunk):
             count = cnt_ref[0, q * per + at * blocks + i // cap]
@@ -308,8 +283,56 @@
             alive = jnp.where(p_slot == i, live, alive)
         alive = jnp.where(p_ae < 9, alive, 0)
         alive_f = alive.astype(F32)
-
-        ur, ui = early if chunks == 1 else spread_own(at)
+        keep = in_window & (alive > 0)
+        ur, ui = spread_own(at)
+        return ur, ui, alive_f, keep
+
+    early = first_part(0) if chunks == 1 else None
+    wait_block(
+        lambda count: many(row_send, row_recv, count, row_ss, row_rs), lambda c: c.wait_recv()
+    )
+    for load in loads[3:]:
+        load.wait()
+
+    def far_copy(peer, inner, slot):
+        return pltpu.make_async_remote_copy(
+            src_ref=far_send.at[peer * per + inner], dst_ref=far_recv.at[slot],
+            send_sem=far_ss, recv_sem=far_rs,
+            device_id=(q * per + inner, peer), device_id_type=MESH,
+        )
+
+    def ownt_copy(peer, slot):
+        return pltpu.make_async_remote_copy(
+            src_ref=ownt_send.at[peer], dst_ref=ownt_recv.at[slot], send_sem=ownt_ss,
+            recv_sem=ownt_rs, device_id=(b, peer), device_id_type=MESH,
+        )
+
+    def send_quarter(peer):
+        def far_start(inner):
+            other = jnp.logical_or(q * per + inner != b, q != peer)
+
+            @pl.when(other)
+            def _():
+                far_copy(peer, inner, b).start()
+
+            @pl.when(jnp.logical_not(other))
+            def _():
+                far_recv[b] = far_send[peer * per + inner]
+
+        loop(per, far_start)
+
+        @pl.when(q != peer)
+        def _():
+            ownt_copy(peer, q).start()
+
+        @pl.when(q == peer)
+        def _():
+            ownt_recv[peer] = ownt_send[peer]
+
+    def work(at):
+        if chunks > 1:
+            prepare(at)
+        ur, ui, alive_f, keep = early if chunks == 1 else first_part(at)
         vr, vi = spread(
             expand_v,
             [
@@ -327,27 +350,21 @@
             ],
             axis=1,
         )
-        residual = jnp.where(
-            in_window & (alive > 0), correlation - obsf[...], 0.0
-        ).astype(BF)
+        residual = jnp.where(keep, correlation - obsf[...], 0.0).astype(BF)
         adj = jnp.dot(residual, kept[...], preferred_element_type=F32).astype(BF).astype(F32)
         ar, ai = adj[:, :NF], adj[:, NF:]
 
-        def reduce(matrix, real, imag):
+        def halves(real, imag):
             terms = jnp.concatenate([real, imag], axis=1)
-            top = terms.astype(BF)
-            rest = (terms - top.astype(F32)).astype(BF)
-            return jnp.dot(matrix, top, preferred_element_type=F32) + jnp.dot(
-                matrix, rest, preferred_element_type=F32
-            )
-
-        grad = jnp.concatenate(
-            [
-                reduce(sum_e, ar * vr - ai * vi, ar * vi + ai * vr),
-                reduce(sum_a, ar * ur + ai * ui, ar * ui - ai * ur),
-            ],
+            upper = terms.astype(BF)
+            return [upper, (terms - upper.astype(F32)).astype(BF)]
+
+        terms = jnp.concatenate(
+            halves(ar * vr - ai * vi, ar * vi + ai * vr)
+            + halves(ar * ur + ai * ui, ar * ui - ai * ur),
             axis=0,
         )
+        grad = jnp.dot(sums, terms, preferred_element_type=F32)
         top = grad.astype(BF)
         rest = (grad - top.astype(F32)).astype(BF)
         stacked = jnp.concatenate([top, rest], axis=0)
@@ -380,22 +397,17 @@
             send_quarter(peer)
 
     def scatter(matrix, values):
-        return lax.dot_general(
-            matrix, values, (((0,), (0,)), ((), ())), preferred_element_type=F32
-        )
+        return jnp.dot(matrix, values, preferred_element_type=F32)
 
     many(ownt_send, ownt_recv, n_q - 1, ownt_ss, ownt_rs).wait_recv()
     own_time = ownt_recv[...].reshape(n_q * item * 8, half)
     own_top = own_time.astype(BF)
     own_rest = (own_time - own_top.astype(F32)).astype(BF)
-    g_mine = g_own[...].reshape(n_b * rows, cols)
-    own_sum = scatter(g_mine, own_top) + scatter(g_mine, own_rest)
+    own_sum = scatter(g_turn[1], own_top) + scatter(g_turn[1], own_rest)
     wait_block(
         lambda count: many(far_send, far_recv, count, far_ss, far_rs), lambda c: c.wait_recv()
     )
-    summed = own_sum + scatter(
-        g_recv[...].reshape(n_b * rows, cols), far_recv[...].reshape(n_b * rows, half)
-    )
+    summed = own_sum + scatter(g_turn[0], far_recv[...].reshape(n_b * rows, half))
     for h in range(2):
         at_row = h * 4 * sta
         out_ref[:, :, h * half : (h + 1) * half] = summed[at_row : at_row + 3 * sta].reshape(
@@ -447,6 +459,7 @@
             pltpu.VMEM((n_b, rows, cols), BF),
             pltpu.VMEM((n_b, rows, cols), BF),
             pltpu.VMEM((n_b, rows, cols), BF),
+            pltpu.VMEM((2, cols, n_b * rows), BF),
             pltpu.VMEM((n_q, item * 8, band), BF),
             pltpu.VMEM((n_q, item * 8, band), BF),
             pltpu.VMEM((n_b, rows, band), BF),

time: 19.9 us -> 19.8 us (level)
  no operation moved by 1% of the time
where the time goes in v1:
time: 19.8 us; the launch traced here: 19.6 us
  Pallas kernels  19 us (96%)
  local copies, waits for them, and re-layouts  0.62 us (3%)
    pallas_call x1, Pallas kernels, local(): pl.pallas_call(functools.partial(kernel, n_b, n_q, cap, sta, item, scale)...  19 us
    unnamed x1, local copies, waits for them, and re-layouts  0.62 us

profile of v1, /device:TPU:0, one launch (start us, length us, event | category | flops | bytes accessed | tf_op | source)
XLA Modules:
  0.0 19.6 jit_solution(15559869369064464502)
XLA Ops:
  0.0 19.0 %shard_map.73 = f32[3,16,256]{2,1,0:T(8,128)S(1)} custom-call(bf16[2,3,16,128]{3,2,1,0:T(8,128)(2,1)} %spec_ref.1, bf16[3,3,4,1024]{3,2,1,0:T(4,128)(2,1)} %bitcast.9, s32[2,8]{1,0:T(2,128)} %bitcast.10, s32[2,8]{1,0:T(2,128)} %bitcast.11, s32[1,8]{1,0:T(1,128)} %cnt_in.1, bf16[1024,1024]{1,0:T(8,128)(2,1)} %constant.4.clone.high_ref, ...), custom_call_target="tpu_custom_call" | custom-call | flops 400000000 | bytes 6000000 | tf_op jit(solution)/shard_map/pallas_call | solution.py:445
  19.0 0.6 %copy.9 = f32[256,3,16]{0,2,1:T(8,128)} copy(f32[256,3,16]{0,2,1:T(8,128)S(1)} %bitcast.8) | data formatting | bytes 98304

commit v2 on v1

--- a/solution.py
+++ b/solution.py
@@ -31,7 +31,7 @@
 
 
 def loop(count, body):
-    if count <= 8:
+    if count <= 2:
         for step in range(count):
             body(step)
     else:
@@ -41,13 +41,21 @@
             return carry
 
         lax.fori_loop(0, count, wrapped, 0)
+
+
+def tiles(count, body):
+    def wrapped(step, carry):
+        body(step)
+        return carry
+
+    lax.fori_loop(0, count, wrapped, 0)
 
 
 def kernel(
     n_b, n_q, cap, sta, item, scale,
     spec_ref, obs_ref, own_in, part_in, cnt_in, high_ref, kept_ref,
     out_ref,
-    own_ref, part_ref, cnt_ref, spec, obs, high, kept, obsf,
+    own_ref, part_ref, cnt_ref, spec, obs, high, kept, obsf, corr, adjs,
     g_send, g_recv, g_own, g_turn, own_send, own_recv, row_send, row_recv,
     far_send, far_recv, ownt_send, ownt_recv,
     local_sem, g_ss, g_rs, own_ss, own_rs, row_ss, row_rs, far_ss, far_rs, ownt_ss, ownt_rs,
@@ -96,10 +104,12 @@
             barrier, inc=1, device_id=(wrap(b + 1 + step, n_b), q), device_id_type=MESH
         )
 
-    for step in range(n_q - 1):
+    def greet_band(step):
         pl.semaphore_signal(
             barrier, inc=1, device_id=(b, wrap(q + 1 + step, n_q)), device_id_type=MESH
         )
+
+    loop(n_q - 1, greet_band)
     loop(n_b - 1, greet)
     for load in loads:
         load.start()
@@ -171,8 +181,7 @@
         g_own[...].reshape(n_b * rows, cols), station_rows, preferred_element_type=F32
     ).astype(BF)
     own_send[...] = picked.reshape(n_q, item * 8, band)
-    for step in range(n_q - 1):
-        own_copy(wrap(q + 1 + step, n_q), q).start()
+    loop(n_q - 1, lambda step: own_copy(wrap(q + 1 + step, n_q), q).start())
     own_recv[q] = own_send[q]
 
     p_i = lax.broadcasted_iota(jnp.int32, (prow, 1), 0)
@@ -343,15 +352,21 @@
         cross = jnp.concatenate(
             [(ur * vr + ui * vi) * alive_f, (ui * vr - ur * vi) * alive_f], axis=1
         ).astype(BF)
-        correlation = jnp.concatenate(
-            [
-                jnp.dot(cross, high[:, :LAG], preferred_element_type=F32),
-                jnp.dot(cross, high[:, NT - LAG :], preferred_element_type=F32),
-            ],
-            axis=1,
-        )
-        residual = jnp.where(keep, correlation - obsf[...], 0.0).astype(BF)
-        adj = jnp.dot(residual, kept[...], preferred_element_type=F32).astype(BF).astype(F32)
+
+        def correlate(side):
+            column = pl.ds(pl.multiple_of(side * (NT - LAG), LAG), LAG)
+            into = pl.ds(pl.multiple_of(side * LAG, LAG), LAG)
+            corr[:, into] = jnp.dot(cross, high[:, column], preferred_element_type=F32)
+
+        tiles(2, correlate)
+        residual = jnp.where(keep, corr[...] - obsf[...], 0.0).astype(BF)
+
+        def back(tile):
+            column = pl.ds(pl.multiple_of(tile * LAG, LAG), LAG)
+            adjs[:, column] = jnp.dot(residual, kept[:, column], preferred_element_type=F32)
+
+        tiles(2 * NF // LAG, back)
+        adj = adjs[...].astype(BF).astype(F32)
         ar, ai = adj[:, :NF], adj[:, NF:]
 
         def halves(real, imag):
@@ -370,11 +385,10 @@
         stacked = jnp.concatenate([top, rest], axis=0)
         count = chunk * 16
         first_half = (lax.broadcasted_iota(jnp.int32, (count, half), 0) & 7) < 4
-        for peer in range(n_q):
-            at_col = peer * 2 * half
-            product = jnp.dot(
-                stacked, high[:, at_col : at_col + 2 * half], preferred_element_type=F32
-            )
+
+        def quarter(peer):
+            column = pl.ds(pl.multiple_of(peer * 2 * half, 2 * half), 2 * half)
+            product = jnp.dot(stacked, high[:, column], preferred_element_type=F32)
             product = (product[:count] + product[count:]) * scale
             message = jnp.where(first_half, product[:, :half], product[:, half:])
             ownt_send[peer, pl.ds(at * chunk * 8, chunk * 8), :] = message[: chunk * 8]
@@ -384,6 +398,8 @@
             if chunks == 1:
                 send_quarter(peer)
 
+        tiles(n_q, quarter)
+
     if chunks == 1:
         work(0)
     else:
@@ -393,8 +409,7 @@
             return carry
 
         lax.fori_loop(0, chunks, work_step, 0)
-        for peer in range(n_q):
-            send_quarter(peer)
+        loop(n_q, send_quarter)
 
     def scatter(matrix, values):
         return jnp.dot(matrix, values, preferred_element_type=F32)
@@ -456,6 +471,8 @@
             pltpu.VMEM(high.shape, BF),
             pltpu.VMEM(kept.shape, BF),
             pltpu.VMEM((prow, 2 * LAG), F32),
+            pltpu.VMEM((prow, 2 * LAG), F32),
+            pltpu.VMEM((prow, 2 * NF), F32),
             pltpu.VMEM((n_b, rows, cols), BF),
             pltpu.VMEM((n_b, rows, cols), BF),
             pltpu.VMEM((n_b, rows, cols), BF),

time: 19.8 us -> 20.4 us (1.030)
  Pallas kernels: 19 us -> 19.7 us
    pallas_call x1, Pallas kernels: 19 us -> 19.7 us  [local(): pl.pallas_call(functools.partial(kernel, n_b, n_q, cap, sta, item, scale)...]
where the time goes in v2:
time: 20.4 us; the launch traced here: 20.3 us
  Pallas kernels  19.7 us (97%)
  local copies, waits for them, and re-layouts  0.62 us (3%)
    pallas_call x1, Pallas kernels, local(): pl.pallas_call(functools.partial(kernel, n_b, n_q, cap, sta, item, scale)...  19.7 us
    unnamed x1, local copies, waits for them, and re-layouts  0.62 us

profile of v2, /device:TPU:0, one launch (start us, length us, event | category | flops | bytes accessed | tf_op | source)
XLA Modules:
  0.0 20.3 jit_solution(9363244240059239703)
XLA Ops:
  0.0 19.7 %shard_map.73 = f32[3,16,256]{2,1,0:T(8,128)S(1)} custom-call(bf16[2,3,16,128]{3,2,1,0:T(8,128)(2,1)} %spec_ref.1, bf16[3,3,4,1024]{3,2,1,0:T(4,128)(2,1)} %bitcast.9, s32[2,8]{1,0:T(2,128)} %bitcast.10, s32[2,8]{1,0:T(2,128)} %bitcast.11, s32[1,8]{1,0:T(1,128)} %cnt_in.1, bf16[1024,1024]{1,0:T(8,128)(2,1)} %constant.4.clone.high_ref, ...), custom_call_target="tpu_custom_call" | custom-call | flops 400000000 | bytes 6000000 | tf_op jit(solution)/shard_map/pallas_call | solution.py:460
  19.7 0.6 %copy.9 = f32[256,3,16]{0,2,1:T(8,128)} copy(f32[256,3,16]{0,2,1:T(8,128)S(1)} %bitcast.8) | data formatting | bytes 98304

commit v3 on v1

--- a/solution.py
+++ b/solution.py
@@ -370,18 +370,21 @@
         stacked = jnp.concatenate([top, rest], axis=0)
         count = chunk * 16
         first_half = (lax.broadcasted_iota(jnp.int32, (count, half), 0) & 7) < 4
+        product = jnp.dot(stacked, high[...], preferred_element_type=F32)
+        product = (product[:count] + product[count:]) * scale
         for peer in range(n_q):
             at_col = peer * 2 * half
-            product = jnp.dot(
-                stacked, high[:, at_col : at_col + 2 * half], preferred_element_type=F32
+            message = jnp.where(
+                first_half,
+                product[:, at_col : at_col + half],
+                product[:, at_col + half : at_col + 2 * half],
             )
-            product = (product[:count] + product[count:]) * scale
-            message = jnp.where(first_half, product[:, :half], product[:, half:])
             ownt_send[peer, pl.ds(at * chunk * 8, chunk * 8), :] = message[: chunk * 8]
             far_send[pl.ds(peer * per + at * blocks, blocks)] = (
                 message[chunk * 8 :].astype(BF).reshape(blocks, rows, half)
             )
-            if chunks == 1:
+        if chunks == 1:
+            for peer in range(n_q):
                 send_quarter(peer)
 
     if chunks == 1:

time: 19.8 us -> 19.9 us (level)
  no operation moved by 1% of the time
where the time goes in v3:
time: 19.9 us; the launch traced here: 19.8 us
  Pallas kernels  19.1 us (96%)
  local copies, waits for them, and re-layouts  0.62 us (3%)
    pallas_call x1, Pallas kernels, local(): pl.pallas_call(functools.partial(kernel, n_b, n_q, cap, sta, item, scale)...  19.1 us
    unnamed x1, local copies, waits for them, and re-layouts  0.62 us

profile of v3, /device:TPU:0, one launch (start us, length us, event | category | flops | bytes accessed | tf_op | source)
XLA Modules:
  0.0 19.8 jit_solution(14055762382998028634)
XLA Ops:
  0.0 19.1 %shard_map.73 = f32[3,16,256]{2,1,0:T(8,128)S(1)} custom-call(bf16[2,3,16,128]{3,2,1,0:T(8,128)(2,1)} %spec_ref.1, bf16[3,3,4,1024]{3,2,1,0:T(4,128)(2,1)} %bitcast.9, s32[2,8]{1,0:T(2,128)} %bitcast.10, s32[2,8]{1,0:T(2,128)} %bitcast.11, s32[1,8]{1,0:T(1,128)} %cnt_in.1, bf16[1024,1024]{1,0:T(8,128)(2,1)} %constant.4.clone.high_ref, ...), custom_call_target="tpu_custom_call" | custom-call | flops 400000000 | bytes 6000000 | tf_op jit(solution)/shard_map/pallas_call | solution.py:448
  19.1 0.6 %copy.9 = f32[256,3,16]{0,2,1:T(8,128)} copy(f32[256,3,16]{0,2,1:T(8,128)S(1)} %bitcast.8) | data formatting | bytes 98304
